TPU v7x, 32 devices: a whole 2x2x4 slice. The times are simulated.
32 devices in a mesh: city: 2 (over y), blk: 4 (over z), band: 2 (over x), sub: 2 (over core).
Axes of the slice: x: 2, y: 2, z: 4, core: 2. Of those that a mesh axis runs over, the one named last changes fastest.
Arguments:
- positions: float32 [3, 8192], P(None, ('city', 'blk')), parts along dimension 1, may hold values from -1.25 to 1.25
- angles: float32 [2, 8192], P(None, ('city', 'blk')), parts along dimension 1, may hold values from -3.140625 to 3.140625
- area: float32 [1, 8192], P(None, ('city', 'blk')), parts along dimension 1, may hold values from 0.25 to 1
- vis_list: int32 [32, 8], P(('city', 'blk'), 'sub'), parts along dimension 0, may hold values from 0 to 15, as said below
- counts: int32 [32], P(('city', 'blk')), parts along dimension 0, may hold values from 1 to 8, as said below
- occl: int32 [32, 8, 16, 256], P(('city', 'blk'), 'sub'), parts along dimension 0, may hold values from 0 to 65535
- direct: float32 [16, 8192], P('band', ('city', 'blk')), parts along dimension 1, may hold values from 0.1 to 2
- reflect: float32 [16, 8192], P('band', ('city', 'blk')), parts along dimension 1, may hold values from 0.25 to 0.9
- band_frac: float32 [16], P('band'), may hold values from 0.02 to 0.2
- temp: float32 [8192], P(('city', 'blk')), parts along dimension 0, may hold values from 0.8 to 1.2
- heat: float32 [8192], P(('city', 'blk')), parts along dimension 0, may hold values from 0.02 to 0.2
Outputs:
- radiosity: float32 [16, 8192], P('band', ('city', 'blk')), parts along dimension 1
- new_temp: float32 [8192], P(('city', 'blk')), parts along dimension 0
There are 2 independent parts, one for each index of `city`. A program takes and returns all parts, laid end to end along the dimension named above; an argument that names none is the same for every part. Nothing has to cross between parts.
Inputs may be any that keep to these rules, and one draw needn't show every extreme that they name: `vis_list`: row block r is held by index r // 4 of blk. Among the slots of the 4 row blocks of one index of blk that one index of sub holds, at most 4 name blocks held by any one index of blk, and for every such group of slots some index of blk holds exactly 4 of them. `counts`: some row block has all 8 slots valid.
All inputs are finite; a program needn't handle non-finite values.
Results may differ from a plain program's by a relative error of at most 0.0003.
Values sent between devices are 32-bit elements; how exact they have to be, the bound alone decides.
A program may use at most 128 MiB of HBM per device.

v0:
```python
import math

import jax
import jax.numpy as jnp
from jax import lax
from jax.sharding import PartitionSpec as P

ITERS = 3


def normals(angles):
    azimuth = angles[0]
    height_angle = 0.5 * angles[1]
    return jnp.stack(
        [
            jnp.cos(height_angle) * jnp.cos(azimuth),
            jnp.cos(height_angle) * jnp.sin(azimuth),
            jnp.sin(height_angle),
        ]
    )


def column_weights(pos_row, normal_row, pos_col, normal_col, area_col, packed):
    delta_x = pos_col[0][:, None] - pos_row[0][None, :]
    delta_y = pos_col[1][:, None] - pos_row[1][None, :]
    delta_z = pos_col[2][:, None] - pos_row[2][None, :]
    dist_sq = delta_x * delta_x + delta_y * delta_y + delta_z * delta_z + area_col[:, None]
    cos_row = jnp.maximum(
        normal_row[0][None, :] * delta_x
        + normal_row[1][None, :] * delta_y
        + normal_row[2][None, :] * delta_z,
        0.0,
    )
    cos_col = jnp.maximum(
        -(
            normal_col[0][:, None] * delta_x
            + normal_col[1][:, None] * delta_y
            + normal_col[2][:, None] * delta_z
        ),
        0.0,
    )
    bit_shift = jnp.arange(16, dtype=jnp.int32)
    visible = (
        jnp.bitwise_and(jnp.right_shift(packed[:, None, :], bit_shift[None, :, None]), 1)
        .reshape(-1, packed.shape[1])
        .astype(jnp.float32)
    )
    return visible * cos_row * cos_col * area_col[:, None] / (math.pi * dist_sq * dist_sq)


def local(positions, angles, area, vis_list, counts, occl, direct, reflect, band_frac, temp, heat):
    block_size = occl.shape[3]
    blocks = vis_list.shape[0]
    listed = vis_list.shape[1]
    row_count = positions.shape[1]
    band_count = direct.shape[0]
    all_pos, all_ang, all_area = (
        lax.all_gather(positions, "blk", axis=1, tiled=True),
        lax.all_gather(angles, "blk", axis=1, tiled=True),
        lax.all_gather(area, "blk", axis=1, tiled=True),
    )
    all_normal = normals(all_ang)
    own_normal = normals(angles)
    entry_ids = lax.axis_index("sub") * listed + jnp.arange(listed, dtype=jnp.int32)
    live_mask = (entry_ids[None, :] < counts[:, None]).astype(jnp.float32)
    block_ids = jnp.arange(blocks, dtype=jnp.int32)
    flat_list = vis_list.reshape(blocks * listed)
    row_pos = positions.reshape(3, blocks, block_size)
    row_normal = own_normal.reshape(3, blocks, block_size)
    col_pos = jnp.take(all_pos.reshape(3, -1, block_size), flat_list, axis=1).reshape(
        3, blocks, listed, block_size
    )
    col_normal = jnp.take(all_normal.reshape(3, -1, block_size), flat_list, axis=1).reshape(
        3, blocks, listed, block_size
    )
    col_area = jnp.take(all_area[0].reshape(-1, block_size), flat_list, axis=0).reshape(
        blocks, listed, block_size
    )
    inner_map = jax.vmap(column_weights, in_axes=(None, None, 1, 1, 0, 0))
    outer_map = jax.vmap(inner_map, in_axes=(1, 1, 1, 1, 0, 0))
    stored = (
        outer_map(row_pos, row_normal, col_pos, col_normal, col_area, occl)
        * live_mask[:, :, None, None]
    )
    partial_total = jnp.sum(stored, axis=(1, 2))
    row_total = lax.psum(partial_total, "sub")
    row_denom = row_total + area[0].reshape(blocks, block_size)
    stored = stored / row_denom[:, None, None, :]
    blk_count = lax.axis_size("blk")
    own_index = lax.axis_index("blk")
    slot_total = blocks * listed
    capacity = (slot_total + blk_count - 1) // blk_count
    all_lists = lax.all_gather(vis_list, "blk", axis=0, tiled=True)
    wanted = all_lists.reshape(blk_count, slot_total)
    holder_of = wanted // blocks
    local_blk = wanted % blocks
    mine = (holder_of == own_index).astype(jnp.int32)
    order_in = jnp.cumsum(mine, axis=1) - 1
    level_ids = jnp.arange(capacity, dtype=jnp.int32)
    matches = (mine[:, :, None] == 1) & (order_in[:, :, None] == level_ids[None, None, :])
    pick_table = jnp.sum(
        (
            (local_blk[:, :, None, None] == block_ids[None, None, None, :]) & matches[:, :, :, None]
        ).astype(jnp.float32),
        axis=1,
    )
    own_holder = flat_list // blocks
    slot_ids = jnp.arange(slot_total, dtype=jnp.int32)
    earlier = jnp.sum(
        (
            (own_holder[:, None] == own_holder[None, :]) & (slot_ids[None, :] < slot_ids[:, None])
        ).astype(jnp.int32),
        axis=1,
    )
    arrival = own_holder * capacity + earlier
    temp_fourth = temp * temp * temp * temp
    emitted = reflect * direct + (1.0 - reflect) * band_frac[:, None] * temp_fourth[None, :]
    radiosity = emitted
    for iteration in range(ITERS):
        field_blocks = radiosity.reshape(band_count, blocks, block_size)
        outgoing = jnp.einsum(
            "tqr,brj->tqbj", pick_table, field_blocks, precision=lax.Precision.HIGHEST
        )
        received = lax.all_to_all(outgoing, "blk", split_axis=0, concat_axis=0, tiled=True)
        slot_values = jnp.take(
            received.reshape(blk_count * capacity, band_count, block_size), arrival, axis=0
        ).reshape(blocks, listed, band_count, block_size)
        partial_flux = jnp.einsum(
            "reji,rebj->bri", stored, slot_values, precision=lax.Precision.HIGHEST
        ).reshape(band_count, row_count)
        incoming = lax.psum(partial_flux, "sub")
        radiosity = emitted + reflect * incoming
    net_flux_part = jnp.sum(
        (1.0 - reflect) * (direct + incoming - band_frac[:, None] * temp_fourth[None, :]), axis=0
    )
    net_total = lax.psum(net_flux_part, "band")
    new_temp = temp + heat * net_total
    return (radiosity, new_temp)


def solution(mesh):
    placed = (
        P(None, ("city", "blk")),
        P(None, ("city", "blk")),
        P(None, ("city", "blk")),
        P(("city", "blk"), "sub"),
        P(("city", "blk")),
        P(("city", "blk"), "sub", None, None),
        P("band", ("city", "blk")),
        P("band", ("city", "blk")),
        P("band"),
        P(("city", "blk")),
        P(("city", "blk")),
    )
    return jax.shard_map(
        local,
        mesh=mesh,
        in_specs=placed,
        out_specs=(P("band", ("city", "blk")), P(("city", "blk"))),
        check_vma=False,
    )
```

profile of v0, /device:TPU:0, one launch (start us, length us, event | category | flops | bytes accessed | tf_op | source)
XLA Modules:
  0.0 139.6 jit_solution(6694297546811626575)
XLA Ops:
  0.7 13.8 %all-gather = s32[4,4,4]{2,1,0:T(4,128)S(1)} all-gather(s32[1,4,4]{2,1,0:T(4,128)} %bitcast.86), channel_id=1, replica_groups=mesh['city'=2,'blk'=4,'band'=2,'sub'=2] {'blk'}, dimensions={0}, use_global_device_ids=true | all-gather | bytes 320 | tf_op jit(solution)/shard_map/all_gather | solution.py:93
  14.6 0.2 reduce_window_sum.11
  14.8 0.7 multiply_multiply_fusion.2
  15.5 0.1 convert_reduce_fusion
  15.6 0.9 multiply_add_fusion.3
  16.4 0.9 fusion.38
  17.4 3.4 %all-to-all-start = ((f32[4,4,8,256]{3,1,2,0:T(4,128)}), f32[4,4,8,256]{3,1,2,0:T(4,128)S(1)}, u32[]{:S(2)}, u32[]{:S(2)}) async-start(f32[4,4,8,256]{3,1,2,0:T(4,128)} %fusion.38), calls=%async_computation | async-start | bytes 262144 | tf_op jit(solution)/shard_map/all_to_all | solution.py:124
  20.7 0.8 reshape.365
  21.5 0.8 reshape.368
  22.3 0.7 compare_and_fusion.2
  23.0 13.9 %all_gather.14 = f32[2,4096]{1,0:T(2,128)S(1)} all-gather(f32[2,1024]{1,0:T(2,128)} %param.16), channel_id=1, replica_groups=mesh['city'=2,'blk'=4,'band'=2,'sub'=2] {'blk'}, dimensions={1}, use_global_device_ids=true | all-gather | bytes 40960 | tf_op jit(solution)/shard_map/all_gather | solution.py:59
  36.9 1.0 multiply_reduce_fusion.2
  37.9 13.4 %all_gather.13 = f32[3,4096]{1,0:T(4,128)S(1)} all-gather(f32[3,1024]{1,0:T(4,128)} %param.15), channel_id=1, replica_groups=mesh['city'=2,'blk'=4,'band'=2,'sub'=2] {'blk'}, dimensions={1}, use_global_device_ids=true | all-gather | bytes 61440 | tf_op jit(solution)/shard_map/all_gather | solution.py:58
  51.3 0.9 slice_reduce_fusion.8
  52.2 13.3 %all_gather.15 = f32[1,4096]{1,0:T(1,128)S(1)} all-gather(f32[1,1024]{1,0:T(1,128)} %param.17), channel_id=1, replica_groups=mesh['city'=2,'blk'=4,'band'=2,'sub'=2] {'blk'}, dimensions={1}, use_global_device_ids=true | all-gather | bytes 20480 | tf_op jit(solution)/shard_map/all_gather | solution.py:60
  65.5 0.5 broadcast.460
  66.0 0.7 reduce.49
  66.7 0.6 gather_fusion
  67.3 0.1 gather.16
  67.4 1.0 cosine_multiply_fusion
  68.5 0.6 gather_fusion.3
  69.1 0.6 gather_fusion.2
  69.7 0.1 select_bitcast_fusion.1
  69.8 0.3 slice_reduce_fusion.2
  70.4 0.1 sub.122
  70.5 0.1 sub.126
  70.9 0.2 convert_reduce_fusion.1
  71.1 0.7 compare_convert_fusion
  71.8 6.5 %fusion.33 = f32[4,256]{1,0:T(4,128)S(1)} fusion(f32[4,4]{1,0:T(4,128)S(1)} %compare_convert_fusion, f32[4,4,16,16]{3,2,1,0:T(8,128)S(1)} %broadcast_select_fusion.3, f32[4,4,16,16]{3,2,1,0:T(8,128)S(1)} %mul.322, f32[4,4,16,16]{3,2,1,0:T(8,128)S(1)} %mul.319, f32[4,4,16,16]{3,2,1,0:T(8,128)S(1)} %mul.316, f32[4,256]{1,0:T(4,128)S(1)} %sub.115, ...), kind=kLoop, calls=%fused_computation.60 | loop fusion | flops 34601984 | bytes 405568 | tf_op jit(solution)/shard_map/reduce_sum | solution.py:85
  78.3 0.7 reduce.50
  79.1 2.4 %psum.35 = f32[4,256]{1,0:T(4,128)S(1)} all-reduce(f32[4,256]{1,0:T(4,128)S(1)} %fusion.33), channel_id=1, replica_groups=mesh['city'=2,'blk'=4,'band'=2,'sub'=2] {'sub'}, use_global_device_ids=true, to_apply=%region_4.7 | all-reduce | flops 1024 | bytes 8192 | tf_op jit(solution)/shard_map/psum | solution.py:86
  81.6 6.3 %fusion.2 = f32[4,4,256,256]{3,2,1,0:T(8,128)} fusion(f32[4,256]{1,0:T(4,128)S(1)} %add.165, f32[4,4]{1,0:T(4,128)S(1)} %compare_convert_fusion, f32[4,4,256]{2,1,0:T(4,128)S(1)} %broadcast_select_fusion.4, f32[4,4,256]{2,1,0:T(4,128)S(1)} %mul.294, f32[4,4,256]{2,1,0:T(4,128)S(1)} %mul.291, f32[4,4,256]{2,1,0:T(4,128)S(1)} %mul.288, f32[4,256]{1,0:T(4,128)S(1)} %sub.115, ...), kind=kLoop, calls=%fused_computation.28 | loop fusion | flops 34603008 | bytes 4600896 | tf_op jit(solution)/shard_map/div | solution.py:88
  87.9 0.6 gather_fusion.1
  88.6 4.3 %fusion.56 = f32[4,8,256,1]{2,1,3,0:T(8,128)S(1)} fusion(f32[4,4,8,256]{3,2,1,0:T(8,128)S(1)} %bitcast.72, f32[4,4,256,256]{3,2,1,0:T(8,128)} %fusion.2), kind=kOutput, calls=%fused_computation.143 | convolution fusion | flops 100663296 | bytes 4358144 | tf_op jit(solution)/shard_map/reji,rebj->bri/dot_general | solution.py:128
  92.9 3.4 %psum.36 = f32[8,1024]{1,0:T(8,128)S(1)} all-reduce(f32[8,1024]{1,0:T(8,128)S(1)} %bitcast.79), channel_id=1, replica_groups=mesh['city'=2,'blk'=4,'band'=2,'sub'=2] {'sub'}, use_global_device_ids=true, to_apply=%region_5.8 | all-reduce | flops 8192 | bytes 65536 | tf_op jit(solution)/shard_map/psum | solution.py:131
  96.3 0.3 fusion.36
  96.6 10.7 %all_to_all.15 = f32[4,4,8,256]{3,1,2,0:T(4,128)S(1)} all-to-all(f32[4,4,8,256]{3,1,2,0:T(4,128)S(1)} %fusion.36), channel_id=1, replica_groups=mesh['city'=2,'blk'=4,'band'=2,'sub'=2] {'blk'}, dimensions={0} | all-to-all | bytes 262144 | tf_op jit(solution)/shard_map/all_to_all | solution.py:124
  107.3 0.6 gather_fusion.4
  108.0 4.3 %fusion.57 = f32[4,8,256,1]{2,1,3,0:T(8,128)S(1)} fusion(f32[4,4,8,256]{3,2,1,0:T(8,128)S(1)} %bitcast.73, f32[4,4,256,256]{3,2,1,0:T(8,128)} %fusion.2), kind=kOutput, calls=%fused_computation.144 | convolution fusion | flops 100663296 | bytes 4358144 | tf_op jit(solution)/shard_map/reji,rebj->bri/dot_general | solution.py:128
  112.3 3.4 %psum.37 = f32[8,1024]{1,0:T(8,128)S(1)} all-reduce(f32[8,1024]{1,0:T(8,128)S(1)} %bitcast.80), channel_id=1, replica_groups=mesh['city'=2,'blk'=4,'band'=2,'sub'=2] {'sub'}, use_global_device_ids=true, to_apply=%region_6.9 | all-reduce | flops 8192 | bytes 65536 | tf_op jit(solution)/shard_map/psum | solution.py:131
  115.7 0.3 fusion.34
  116.0 9.1 %all_to_all.16 = f32[4,4,8,256]{3,1,2,0:T(4,128)S(1)} all-to-all(f32[4,4,8,256]{3,1,2,0:T(4,128)S(1)} %fusion.34), channel_id=1, replica_groups=mesh['city'=2,'blk'=4,'band'=2,'sub'=2] {'blk'}, dimensions={0} | all-to-all | bytes 262144 | tf_op jit(solution)/shard_map/all_to_all | solution.py:124
  125.1 0.6 gather_fusion.5
  125.8 4.3 %fusion.58 = f32[4,8,256,1]{2,1,3,0:T(8,128)S(1)} fusion(f32[4,4,8,256]{3,2,1,0:T(8,128)S(1)} %bitcast.71, f32[4,4,256,256]{3,2,1,0:T(8,128)} %fusion.2), kind=kOutput, calls=%fused_computation.145 | convolution fusion | flops 100663296 | bytes 4358144 | tf_op jit(solution)/shard_map/reji,rebj->bri/dot_general | solution.py:128
  130.0 3.4 %psum.38 = f32[8,1024]{1,0:T(8,128)S(1)} all-reduce(f32[8,1024]{1,0:T(8,128)S(1)} %bitcast.78), channel_id=1, replica_groups=mesh['city'=2,'blk'=4,'band'=2,'sub'=2] {'sub'}, use_global_device_ids=true, to_apply=%region_7.10 | all-reduce | flops 8192 | bytes 65536 | tf_op jit(solution)/shard_map/psum | solution.py:131
  133.5 0.6 multiply_reduce_fusion
  134.1 4.9 %psum.39 = f32[1024]{0:T(1024)S(1)} all-reduce(f32[1024]{0:T(1024)S(1)} %get-tuple-element.20), channel_id=1, replica_groups=mesh['city'=2,'blk'=4,'band'=2,'sub'=2] {'band'}, use_global_device_ids=true, to_apply=%region_9.12 | all-reduce | flops 1024 | bytes 8192 | tf_op jit(solution)/shard_map/psum | solution.py:136
  139.0 0.6 multiply_add_fusion.4
  (61 shorter events, 1.4 us)
Async XLA Ops:
  0.6 77.6 %copy-start.3 = (f32[1,1024]{1,0:T(1,128)S(1)}, f32[1,1024]{1,0:T(1,128)}, u32[]{:S(2)}) copy-start(f32[1,1024]{1,0:T(1,128)} %param.17) | copy-start | bytes 12292
  0.6 81.0 %copy-start = (s32[4,4,16,256]{3,2,1,0:T(8,128)S(1)}, s32[4,4,16,256]{3,2,1,0:T(8,128)}, u32[]{:S(2)}) copy-start(s32[4,4,16,256]{3,2,1,0:T(8,128)} %param.20) | copy-start | bytes 786436
  17.4 70.5 %all-to-all-start = ((f32[4,4,8,256]{3,1,2,0:T(4,128)}), f32[4,4,8,256]{3,1,2,0:T(4,128)S(1)}, u32[]{:S(2)}, u32[]{:S(2)}) async-start(f32[4,4,8,256]{3,1,2,0:T(4,128)} %fusion.38), calls=%async_computation | async-start | bytes 262144 | tf_op jit(solution)/shard_map/all_to_all | solution.py:124
  81.6 14.7 %copy-start.1 = (f32[8,1024]{1,0:T(8,128)S(1)}, f32[8,1024]{1,0:T(8,128)}, u32[]{:S(2)}) copy-start(f32[8,1024]{1,0:T(8,128)} %param.22) | copy-start | bytes 98308
  107.9 25.5 %copy-start.2 = (f32[8,1024]{1,0:T(8,128)S(1)}, f32[8,1024]{1,0:T(8,128)}, u32[]{:S(2)}) copy-start(f32[8,1024]{1,0:T(8,128)} %param.21) | copy-start | bytes 98308
  107.9 25.5 %copy-start.6 = (f32[8]{0:T(128)S(1)}, f32[8]{0:T(128)}, u32[]{:S(2)}) copy-start(f32[8]{0:T(128)} %param.23) | copy-start | bytes 100
  108.0 31.1 %copy-start.4 = (f32[1024]{0:T(1024)S(1)}, f32[1024]{0:T(1024)}, u32[]{:S(2)}) copy-start(f32[1024]{0:T(1024)} %param.24) | copy-start | bytes 12292
  108.0 31.1 %copy-start.5 = (f32[1024]{0:T(1024)S(1)}, f32[1024]{0:T(1024)}, u32[]{:S(2)}) copy-start(f32[1024]{0:T(1024)} %param.25) | copy-start | bytes 12292
where the time goes:
time: 141 us; the launch traced here: 140 us
  blocking collectives  91.7 us (65%)
  other arithmetic  21.4 us (15%)
  matrix products  14.3 us (10%)
  local copies, waits for them, and re-layouts  7.68 us (5%)
  starting transfers between devices  3.38 us (2%)
    all_to_all x2, blocking collectives, local(): lax.all_to_all(outgoing, 'blk', split_axis=0, concat_axis=0, tiled=True)  19.8 us
    all_gather x1, blocking collectives, local(): lax.all_gather(angles, 'blk', axis=1, tiled=True)  13.9 us
    all_gather x1, blocking collectives, local(): all_lists = lax.all_gather(vis_list, 'blk', axis=0, tiled=True)  13.8 us
    all_gather x1, blocking collectives, local(): lax.all_gather(positions, 'blk', axis=1, tiled=True)  13.4 us
    all_gather x1, blocking collectives, local(): lax.all_gather(area, 'blk', axis=1, tiled=True)  13.3 us
    dot_general x3, matrix products, local(): jnp.einsum('reji,rebj->bri', stored, slot_values, precision=lax.Precision...  12.9 us
    psum x3, blocking collectives, local(): incoming = lax.psum(partial_flux, 'sub')  10.2 us
    reduce_sum x1, other arithmetic, local(): partial_total = jnp.sum(stored, axis=(1, 2))  6.45 us
  transfers between devices with their start and end apart: 1, of which 0 were waited for; matrix products, arithmetic and copies ran while one was open for 17% of the time, Pallas kernels for 0%

commit v1 on v0

v1 whole, which is shorter than its diff:
```python
import functools
import math

import jax
import jax.numpy as jnp
from jax import lax
from jax.experimental import pallas as pl
from jax.experimental.pallas import tpu as pltpu
from jax.sharding import PartitionSpec as P

ITERS = 3
MESH = pl.DeviceIdType.MESH


def split3(x):
    hi = x.astype(jnp.bfloat16).astype(jnp.float32)
    rest = x - hi
    mid = rest.astype(jnp.bfloat16).astype(jnp.float32)
    return hi, mid, rest - mid


def kernel(
    sizes,
    pos_ref, ang_ref, area_ref, vis_ref, counts_ref, occl_ref, direct_ref, reflect_ref, frac_ref, temp_ref, heat_ref,
    out_ref, newt_ref,
    geo, nrm, coef, rhs, w_hi, w_lo, words, vis_v, vis_s, last, net,
    send_sem, recv_sem, loc_sem,
    *fields,
):
    n_blk, n_band, n_sub, blocks, listed, size = sizes
    half = blocks // n_sub
    slots = listed * n_sub
    chunk = size // 16
    z = lax.axis_index("blk")
    band = lax.axis_index("band")
    sub = lax.axis_index("sub")
    peers = [lax.rem(z + d, n_blk) for d in range(1, n_blk)]
    sources = [lax.rem(z - d + n_blk, n_blk) for d in range(1, n_blk)]
    mates = [
        (lax.rem(band + d, n_band), lax.rem(sub + s, n_sub))
        for d in range(n_band) for s in range(n_sub) if d or s
    ]
    sibling = {"sub": n_sub - 1 - sub}
    started = []

    def send(src, dst, where):
        k = len(started)
        copy = pltpu.make_async_remote_copy(
            src_ref=src, dst_ref=dst, send_sem=send_sem.at[k], recv_sem=recv_sem.at[k],
            device_id=where, device_id_type=MESH,
        )
        copy.start()
        started.append(copy)
        return copy

    barrier = pltpu.get_barrier_semaphore()
    for peer in peers:
        pl.semaphore_signal(barrier, inc=1, device_id={"blk": peer}, device_id_type=MESH)
    for mate in mates:
        pl.semaphore_signal(barrier, inc=1, device_id={"band": mate[0], "sub": mate[1]}, device_id_type=MESH)

    own_words = pltpu.make_async_copy(occl_ref.at[pl.ds(sub * half, half)], words.at[sub], loc_sem.at[0])
    own_words.start()
    vis_v[sub] = vis_ref[...]

    pos = pos_ref[...]
    ang = ang_ref[...]
    azimuth = ang[0:1]
    height = 0.5 * ang[1:2]
    cos_h = jnp.cos(height)
    normal = jnp.concatenate([cos_h * jnp.cos(azimuth), cos_h * jnp.sin(azimuth), jnp.sin(height)], axis=0)
    nrm[...] = normal
    area = area_ref[...]
    scaled = normal * (area * (1.0 / math.pi))
    dist = jnp.sum(pos * pos, axis=0, keepdims=True) + area
    shift = -jnp.sum(scaled * pos, axis=0, keepdims=True)
    for b in range(blocks):
        at = z * blocks + b
        lanes = slice(b * size, (b + 1) * size)
        geo[at, 0:3, :] = pos[:, lanes]
        geo[at, 3:6, :] = scaled[:, lanes]
        geo[at, 6:7, :] = dist[:, lanes]
        geo[at, 7:8, :] = shift[:, lanes]

    pl.semaphore_wait(barrier, len(peers) + len(mates))

    mine = pl.ds(z * blocks + sub * half, half)
    geo_in = [send(geo.at[mine], geo.at[mine], {"blk": peer}) for peer in peers]
    vis_in = send(vis_v.at[sub], vis_v.at[sub], sibling)
    words_in = send(occl_ref.at[pl.ds((n_sub - 1 - sub) * half, half)], words.at[sub], sibling)

    bands = direct_ref.shape[0]
    row = lax.broadcasted_iota(jnp.int32, (bands, 1), 0)
    frac = jnp.zeros((bands, 1), jnp.float32)
    for b in range(frac_ref.shape[0]):
        frac = jnp.where(row == b, frac_ref[b], frac)
    temp = temp_ref[...]
    temp2 = temp * temp
    black = frac * (temp2 * temp2)
    reflect = reflect_ref[...]
    emitted = reflect * direct_ref[...] + (1.0 - reflect) * black
    for b in range(blocks):
        fields[0][z * blocks + b] = emitted[:, b * size:(b + 1) * size]
    field_in = [send(fields[0].at[mine], fields[0].at[mine], {"blk": peer}) for peer in peers]

    for rr in range(half):
        lanes = pl.ds(pl.multiple_of((sub * half + rr) * size, size), size)
        pos_row = pos_ref[:, lanes]
        normal_row = nrm[:, lanes]
        coef[...] = jnp.zeros_like(coef)
        coef[0:3, 0:size] = normal_row
        coef[3:6, size:2 * size] = pos_row
        coef[7:8, size:2 * size] = jnp.ones((1, size), jnp.float32)
        coef[0:3, 2 * size:3 * size] = -2.0 * pos_row
        coef[6:7, 2 * size:3 * size] = jnp.ones((1, size), jnp.float32)
        hi, mid, low = split3(coef[...])
        parts = split3(jnp.concatenate([
            -jnp.sum(pos_row * normal_row, axis=0, keepdims=True),
            jnp.zeros((1, size), jnp.float32),
            jnp.sum(pos_row * pos_row, axis=0, keepdims=True),
        ], axis=1))
        const = jnp.concatenate(list(parts) + [jnp.zeros((5, 3 * size), jnp.float32)], axis=0)
        full = jnp.concatenate([hi, mid, low, hi, mid, hi, const, jnp.zeros_like(const)], axis=0)
        rhs[rr] = full.astype(jnp.bfloat16)

    def forward(copies, place):
        passed = []
        for copy, source in zip(copies, sources):
            copy.wait_recv()
            region = place(pl.ds(source * blocks + sub * half, half))
            passed.append(send(region, region, sibling))
        return passed

    vis_in.wait_recv()
    to_smem = pltpu.make_async_copy(vis_v, vis_s, loc_sem.at[1])
    to_smem.start()
    geo_passed = forward(geo_in, lambda region: geo.at[region])
    to_smem.wait()
    own_words.wait()
    words_in.wait_recv()
    for copy in geo_passed:
        copy.wait_recv()

    bit = jnp.left_shift(1, lax.broadcasted_iota(jnp.int32, (16, 1), 0))
    geo_row = lax.broadcasted_iota(jnp.int32, (8, 1), 0)
    is_scaled = ((geo_row >= 3) & (geo_row < 6)) | (geo_row == 7)
    ones = jnp.ones((8, size), jnp.float32)

    def named(rr, e):
        return vis_s[e // listed, sub * half + rr, e % listed]

    def weights(rr):
        valid = counts_ref[sub * half + rr]

        def tile(e, total):
            live = jnp.where(e < valid, 1.0, 0.0)
            column = geo[named(rr, e)] * jnp.where(is_scaled, live, 1.0)
            hi, mid, low = split3(column)
            lhs = jnp.concatenate([hi, hi, hi, mid, mid, low, ones, jnp.zeros_like(ones)], axis=0)
            lhs = jnp.transpose(lhs).astype(jnp.bfloat16)
            side = rhs[rr]
            for q in range(chunk // 4):
                both = jnp.dot(lhs[q * 64:(q + 1) * 64], side, preferred_element_type=jnp.float32)
                for k in range(4):
                    word = words[e // listed, rr, e % listed, pl.ds(q * 4 + k, 1), :]
                    seen = jnp.bitwise_and(word, bit) != 0
                    lines = slice(k * 16, (k + 1) * 16)
                    cos_row = jnp.where(seen, jnp.maximum(both[lines, 0:size], 0.0), 0.0)
                    cos_col = jnp.maximum(both[lines, size:2 * size], 0.0)
                    square = both[lines, 2 * size:3 * size]
                    square = square * square
                    inverse = pl.reciprocal(square, approx=True)
                    inverse = inverse * (2.0 - square * inverse)
                    w = (cos_row * cos_col) * inverse
                    total = total + (w[0:8] + w[8:16])
                    top = w.astype(jnp.bfloat16)
                    at = pl.ds(pl.multiple_of(e * size, size) + (q * 64 + k * 16), 16)
                    w_hi[rr, at, :] = top
                    w_lo[rr, at, :] = (w - top.astype(jnp.float32)).astype(jnp.bfloat16)
            return total

        total = lax.fori_loop(0, slots, tile, jnp.zeros((8, size), jnp.float32))
        return jnp.sum(total, axis=0, keepdims=True)

    totals = []
    arrived = None
    for rr in range(half):
        totals.append(weights(rr))
        if arrived is None:
            arrived = forward(field_in, lambda region: fields[0].at[region])

    inverse_denom = []
    for rr in range(half):
        lanes = pl.ds(pl.multiple_of((sub * half + rr) * size, size), size)
        inverse_denom.append(1.0 / (totals[rr] + area_ref[:, lanes]))

    waiting = arrived
    for step in range(ITERS):
        for copy in waiting:
            copy.wait_recv()
        waiting, hops = [], []
        for rr in range(half):
            field = jnp.concatenate([fields[step][named(rr, e)] for e in range(slots)], axis=1)
            top = field.astype(jnp.bfloat16).astype(jnp.float32)
            both = jnp.concatenate([top, field - top], axis=0).astype(jnp.bfloat16)
            first = jnp.dot(both, w_hi[rr], preferred_element_type=jnp.float32)
            second = jnp.dot(top.astype(jnp.bfloat16), w_lo[rr], preferred_element_type=jnp.float32)
            incoming = (first[0:bands] + first[bands:] + second) * inverse_denom[rr]
            lanes = pl.ds(pl.multiple_of((sub * half + rr) * size, size), size)
            own_reflect = reflect_ref[:, lanes]
            value = fields[0][z * blocks + sub * half + rr] + own_reflect * incoming
            if step < ITERS - 1:
                at = z * blocks + sub * half + rr
                fields[step + 1][at] = value
                region = fields[step + 1].at[pl.ds(at, 1)]
                for peer, source in zip(peers, sources):
                    hops.append((send(region, region, {"blk": peer}), source * blocks + sub * half + rr))
                waiting.append(send(region, region, sibling))
            else:
                own_temp = temp_ref[:, lanes]
                own_temp2 = own_temp * own_temp
                gain = (1.0 - own_reflect) * (
                    direct_ref[:, lanes] + incoming - frac * (own_temp2 * own_temp2)
                )
                last[sub * half + rr] = value
                region = last.at[pl.ds(sub * half + rr, 1)]
                waiting.append(send(region, region, sibling))
                net[band, sub, rr:rr + 1, :] = jnp.sum(gain, axis=0, keepdims=True)
        for copy, at in hops:
            copy.wait_recv()
            region = fields[step + 1].at[pl.ds(at, 1)]
            waiting.append(send(region, region, sibling))

    for mate in mates:
        waiting.append(send(net.at[band, sub], net.at[band, sub], {"band": mate[0], "sub": mate[1]}))
    for copy in waiting:
        copy.wait_recv()
    for b in range(blocks):
        lanes = slice(b * size, (b + 1) * size)
        out_ref[:, lanes] = last[b]
        flux = net[0, b // half, b % half:b % half + 1, :]
        for other in range(1, n_band):
            flux = flux + net[other, b // half, b % half:b % half + 1, :]
        newt_ref[:, lanes] = temp_ref[:, lanes] + heat_ref[:, lanes] * flux
    for copy in started:
        copy.wait_send()


def local(axes, positions, angles, area, vis_list, counts, occl, direct, reflect, band_frac, temp, heat):
    n_blk, n_band, n_sub = axes
    size = occl.shape[3]
    blocks, listed = vis_list.shape
    half = blocks // n_sub
    rows = positions.shape[1]
    band_count = direct.shape[0]
    bands = -(-band_count // 8) * 8
    if bands != band_count:
        direct = jnp.pad(direct, ((0, bands - band_count), (0, 0)))
        reflect = jnp.pad(reflect, ((0, bands - band_count), (0, 0)), constant_values=1.0)
    total_blocks = n_blk * blocks
    slots = listed * n_sub
    copies = (
        (n_blk - 1) * 4 + 2 + (ITERS - 1) * half * (2 * (n_blk - 1) + 1) + half + n_band * n_sub - 1
    )
    vmem = pl.BlockSpec(memory_space=pltpu.VMEM)
    smem = pl.BlockSpec(memory_space=pltpu.SMEM)
    out, new_temp = pl.pallas_call(
        functools.partial(kernel, (n_blk, n_band, n_sub, blocks, listed, size)),
        out_shape=(
            jax.ShapeDtypeStruct((bands, rows), jnp.float32),
            jax.ShapeDtypeStruct((1, rows), jnp.float32),
        ),
        in_specs=[vmem, vmem, vmem, vmem, smem, pl.BlockSpec(memory_space=pl.ANY), vmem, vmem, smem, vmem, vmem],
        out_specs=(vmem, vmem),
        scratch_shapes=[
            pltpu.VMEM((total_blocks, 8, size), jnp.float32),
            pltpu.VMEM((3, rows), jnp.float32),
            pltpu.VMEM((8, 3 * size), jnp.float32),
            pltpu.VMEM((half, 64, 3 * size), jnp.bfloat16),
            pltpu.VMEM((half, slots * size, size), jnp.bfloat16),
            pltpu.VMEM((half, slots * size, size), jnp.bfloat16),
            pltpu.VMEM((n_sub, half, listed, size // 16, size), jnp.int32),
            pltpu.VMEM((n_sub, blocks, listed), jnp.int32),
            pltpu.SMEM((n_sub, blocks, listed), jnp.int32),
            pltpu.VMEM((blocks, bands, size), jnp.float32),
            pltpu.VMEM((n_band, n_sub, half, size), jnp.float32),
            pltpu.SemaphoreType.DMA((copies,)),
            pltpu.SemaphoreType.DMA((copies,)),
            pltpu.SemaphoreType.DMA((2,)),
        ]
        + [pltpu.VMEM((total_blocks, bands, size), jnp.float32)] * ITERS,
        compiler_params=pltpu.CompilerParams(
            collective_id=0, has_side_effects=True, vmem_limit_bytes=40 * 1024 * 1024
        ),
    )(positions, angles, area, vis_list, counts, occl, direct, reflect, band_frac, temp[None, :], heat[None, :])
    return out[:band_count], new_temp.reshape(rows)


def solution(mesh):
    placed = (
        P(None, ("city", "blk")),
        P(None, ("city", "blk")),
        P(None, ("city", "blk")),
        P(("city", "blk"), "sub"),
        P(("city", "blk")),
        P(("city", "blk"), "sub", None, None),
        P("band", ("city", "blk")),
        P("band", ("city", "blk")),
        P("band"),
        P(("city", "blk")),
        P(("city", "blk")),
    )
    axes = (mesh.shape["blk"], mesh.shape["band"], mesh.shape["sub"])
    return jax.shard_map(
        functools.partial(local, axes),
        mesh=mesh,
        in_specs=placed,
        out_specs=(P("band", ("city", "blk")), P(("city", "blk"))),
        check_vma=False,
    )
```

time: 141 us -> 39.1 us (0.28)
  blocking collectives: 91.7 us -> 0 us
  Pallas kernels: 0 us -> 30.1 us
  other arithmetic: 21.4 us -> 0 us
  matrix products: 14.3 us -> 0 us
  starting transfers between devices: 3.38 us -> 0 us
    all_gather x4 -> x0, blocking collectives: 54.4 us -> none  [the longest x1 13.9 us: local(): lax.all_gather(angles, 'blk', axis=1, tiled=True)]
    pallas_call x0 -> x1, Pallas kernels: none -> 30.1 us  [local(): pl.pallas_call(functools.partial(kernel, (n_blk, n_band, n_sub, blocks, l...]
    all_to_all x2 -> x0, blocking collectives: 19.8 us -> none  [local(): lax.all_to_all(outgoing, 'blk', split_axis=0, concat_axis=0, tiled=True)]
    psum x5 -> x0, blocking collectives: 17.6 us -> none  [the longest x3 10.2 us: local(): incoming = lax.psum(partial_flux, 'sub')]
    dot_general x6 -> x0, matrix products: 14.3 us -> none  [the longest x3 12.9 us: local(): jnp.einsum('reji,rebj->bri', stored, slot_values, precision=lax.Precision...]
    unnamed x14 -> x24, local copies, waits for them, and re-layouts: 0.04 us -> 7.81 us
    reduce_sum x4 -> x0, other arithmetic: 7.36 us -> none  [the longest x1 6.45 us: local(): partial_total = jnp.sum(stored, axis=(1, 2))]
    div x1 -> x0, other arithmetic: 6.26 us -> none  [local(): stored = stored / row_denom[:, None, None, :]]
  transfers between devices with their start and end apart: 1 -> 0, of which waited for: 0 -> 0; matrix products, arithmetic and copies ran while one was open for 17% -> 0% of each run, Pallas kernels for 0% -> 0%
where the time goes in v1:
time: 39.1 us; the launch traced here: 38.6 us
  Pallas kernels  30.1 us (77%)
  local copies, waits for them, and re-layouts  7.81 us (20%)
  between operations  0.68 us (2%)
    pallas_call x1, Pallas kernels, local(): pl.pallas_call(functools.partial(kernel, (n_blk, n_band, n_sub, blocks, l...  30.1 us
    unnamed x24, local copies, waits for them, and re-layouts  7.81 us

profile of v1, /device:TPU:0, one launch (start us, length us, event | category | flops | bytes accessed | tf_op | source)
XLA Modules:
  0.0 38.6 jit_solution(12562875132015084443)
XLA Ops:
  0.6 0.0 copy-start.8
  0.6 0.0 copy-start.9
  0.7 0.0 copy-start.10
  0.7 0.7 %copy-done.8 = s32[4,4]{1,0:T(4,128)S(1)} copy-done((s32[4,4]{1,0:T(4,128)S(1)}, s32[4,4]{1,0:T(4,128)}, u32[]{:S(2)}) %copy-start.8) | copy-done | bytes 88
  1.3 0.0 copy-done.9
  1.3 0.0 copy-done.10
  1.3 0.0 copy-start
  1.3 0.9 %copy-done = s32[4,4,16,256]{3,2,1,0:T(8,128)S(1)} copy-done((s32[4,4,16,256]{3,2,1,0:T(8,128)S(1)}, s32[4,4,16,256]{3,2,1,0:T(8,128)}, u32[]{:S(2)}) %copy-start) | copy-done | bytes 262168
  2.3 0.0 copy-start.1
  2.3 0.8 %copy-done.1 = f32[8,1024]{1,0:T(8,128)S(1)} copy-done((f32[8,1024]{1,0:T(8,128)S(1)}, f32[8,1024]{1,0:T(8,128)}, u32[]{:S(2)}) %copy-start.1) | copy-done | bytes 32792
  3.0 0.0 copy-start.2
  3.0 0.8 %copy-done.2 = f32[8,1024]{1,0:T(8,128)S(1)} copy-done((f32[8,1024]{1,0:T(8,128)S(1)}, f32[8,1024]{1,0:T(8,128)}, u32[]{:S(2)}) %copy-start.2) | copy-done | bytes 32792
  3.8 0.0 copy-start.3
  3.8 0.7 %copy-done.3 = f32[3,1024]{1,0:T(4,128)S(1)} copy-done((f32[3,1024]{1,0:T(4,128)S(1)}, f32[3,1024]{1,0:T(4,128)}, u32[]{:S(2)}) %copy-start.3) | copy-done | bytes 12312
  4.5 0.0 copy-start.4
  4.5 0.7 %copy-done.4 = f32[2,1024]{1,0:T(2,128)S(1)} copy-done((f32[2,1024]{1,0:T(2,128)S(1)}, f32[2,1024]{1,0:T(2,128)}, u32[]{:S(2)}) %copy-start.4) | copy-done | bytes 8216
  5.2 0.0 copy-start.5
  5.2 0.7 %copy-done.5 = f32[1,1024]{1,0:T(1,128)S(1)} copy-done((f32[1,1024]{1,0:T(1,128)S(1)}, f32[1,1024]{1,0:T(1,128)}, u32[]{:S(2)}) %copy-start.5) | copy-done | bytes 4120
  5.9 0.0 copy-start.6
  5.9 0.7 %copy-done.6 = f32[1024]{0:T(1024)S(1)} copy-done((f32[1024]{0:T(1024)S(1)}, f32[1024]{0:T(1024)}, u32[]{:S(2)}) %copy-start.6) | copy-done | bytes 4120
  6.6 0.0 copy-start.7
  6.6 0.7 %copy-done.7 = f32[1024]{0:T(1024)S(1)} copy-done((f32[1024]{0:T(1024)S(1)}, f32[1024]{0:T(1024)}, u32[]{:S(2)}) %copy-start.7) | copy-done | bytes 4120
  7.3 30.1 %shard_map.122 = (f32[8,1024]{1,0:T(8,128)S(1)}, f32[1,1024]{1,0:T(1,128)S(1)}) custom-call(f32[3,1024]{1,0:T(4,128)S(1)} %copy-done.3, f32[2,1024]{1,0:T(2,128)S(1)} %copy-done.4, f32[1,1024]{1,0:T(1,128)S(1)} %copy-done.5, s32[4,4]{1,0:T(4,128)S(1)} %copy-done.8, s32[4]{0:T(128)S(1)} %copy-done.9, s32[4,4,16,256]{3,2,1,0:T(8,128)S(1)} %copy-done, ...), custom_call_target="tpu_custom_call" | custom-call | tf_op jit(solution)/shard_map/pallas_call | solution.py:267
  37.3 0.6 %copy.15 = f32[8,1024]{1,0:T(8,128)} copy(f32[8,1024]{1,0:T(8,128)S(1)} %get-tuple-element.8) | data formatting | bytes 65536
  38.0 0.6 %copy.16 = f32[1024]{0:T(1024)} copy(f32[1024]{0:T(1024)S(1)} %bitcast.5) | data formatting | bytes 8192
Async XLA Ops:
  0.6 0.7 %copy-start.8 = (s32[4,4]{1,0:T(4,128)S(1)}, s32[4,4]{1,0:T(4,128)}, u32[]{:S(2)}) copy-start(s32[4,4]{1,0:T(4,128)} %vis_ref.1) | copy-start | bytes 196
  0.6 0.7 %copy-start.9 = (s32[4]{0:T(128)S(1)}, s32[4]{0:T(128)}, u32[]{:S(2)}) copy-start(s32[4]{0:T(128)} %counts_ref.1) | copy-start | bytes 52
  0.7 0.7 %copy-start.10 = (f32[8]{0:T(128)S(1)}, f32[8]{0:T(128)}, u32[]{:S(2)}) copy-start(f32[8]{0:T(128)} %frac_ref.1) | copy-start | bytes 100
  1.3 1.0 %copy-start = (s32[4,4,16,256]{3,2,1,0:T(8,128)S(1)}, s32[4,4,16,256]{3,2,1,0:T(8,128)}, u32[]{:S(2)}) copy-start(s32[4,4,16,256]{3,2,1,0:T(8,128)} %occl_ref.1) | copy-start | bytes 786436
  2.3 0.8 %copy-start.1 = (f32[8,1024]{1,0:T(8,128)S(1)}, f32[8,1024]{1,0:T(8,128)}, u32[]{:S(2)}) copy-start(f32[8,1024]{1,0:T(8,128)} %direct_ref.1) | copy-start | bytes 98308
  3.0 0.8 %copy-start.2 = (f32[8,1024]{1,0:T(8,128)S(1)}, f32[8,1024]{1,0:T(8,128)}, u32[]{:S(2)}) copy-start(f32[8,1024]{1,0:T(8,128)} %reflect_ref.1) | copy-start | bytes 98308
  3.8 0.7 %copy-start.3 = (f32[3,1024]{1,0:T(4,128)S(1)}, f32[3,1024]{1,0:T(4,128)}, u32[]{:S(2)}) copy-start(f32[3,1024]{1,0:T(4,128)} %pos_ref.1) | copy-start | bytes 36868
  4.5 0.7 %copy-start.4 = (f32[2,1024]{1,0:T(2,128)S(1)}, f32[2,1024]{1,0:T(2,128)}, u32[]{:S(2)}) copy-start(f32[2,1024]{1,0:T(2,128)} %ang_ref.1) | copy-start | bytes 24580
  5.2 0.7 %copy-start.5 = (f32[1,1024]{1,0:T(1,128)S(1)}, f32[1,1024]{1,0:T(1,128)}, u32[]{:S(2)}) copy-start(f32[1,1024]{1,0:T(1,128)} %area_ref.1) | copy-start | bytes 12292
  5.9 0.7 %copy-start.6 = (f32[1024]{0:T(1024)S(1)}, f32[1024]{0:T(1024)}, u32[]{:S(2)}) copy-start(f32[1024]{0:T(1024)} %param.20) | copy-start | bytes 12292
  6.6 0.7 %copy-start.7 = (f32[1024]{0:T(1024)S(1)}, f32[1024]{0:T(1024)}, u32[]{:S(2)}) copy-start(f32[1024]{0:T(1024)} %param.21) | copy-start | bytes 12292

commit v2 on v1

--- a/solution.py
+++ b/solution.py
@@ -21,8 +21,9 @@
 
 def kernel(
     sizes,
-    pos_ref, ang_ref, area_ref, vis_ref, counts_ref, occl_ref, direct_ref, reflect_ref, frac_ref, temp_ref, heat_ref,
+    pos_in, ang_in, area_in, vis_ref, counts_in, occl_ref, direct_in, reflect_in, frac_in, temp_in, heat_in,
     out_ref, newt_ref,
+    pos_ref, ang_ref, area_ref, counts_ref, direct_ref, reflect_ref, frac_ref, temp_ref, heat_ref,
     geo, nrm, coef, rhs, w_hi, w_lo, words, vis_v, vis_s, last, net,
     send_sem, recv_sem, loc_sem,
     *fields,
@@ -53,22 +54,45 @@
         started.append(copy)
         return copy
 
+    loads = []
+
+    def load(src, dst):
+        copy = pltpu.make_async_copy(src, dst, loc_sem.at[len(loads)])
+        copy.start()
+        loads.append(copy)
+        return copy
+
+    shape_in = [load(ang_in, ang_ref), load(pos_in, pos_ref), load(area_in, area_ref)]
+    vis_load = load(vis_ref, vis_v.at[sub])
+    field_loads = [
+        load(frac_in, frac_ref), load(temp_in, temp_ref), load(direct_in, direct_ref), load(reflect_in, reflect_ref)
+    ]
+    late_loads = [
+        load(occl_ref.at[pl.ds(sub * half, half)], words.at[sub]), load(counts_in, counts_ref), load(heat_in, heat_ref)
+    ]
+
     barrier = pltpu.get_barrier_semaphore()
     for peer in peers:
         pl.semaphore_signal(barrier, inc=1, device_id={"blk": peer}, device_id_type=MESH)
     for mate in mates:
         pl.semaphore_signal(barrier, inc=1, device_id={"band": mate[0], "sub": mate[1]}, device_id_type=MESH)
 
-    own_words = pltpu.make_async_copy(occl_ref.at[pl.ds(sub * half, half)], words.at[sub], loc_sem.at[0])
-    own_words.start()
-    vis_v[sub] = vis_ref[...]
-
+
+    for copy in shape_in:
+        copy.wait()
     pos = pos_ref[...]
     ang = ang_ref[...]
-    azimuth = ang[0:1]
-    height = 0.5 * ang[1:2]
-    cos_h = jnp.cos(height)
-    normal = jnp.concatenate([cos_h * jnp.cos(azimuth), cos_h * jnp.sin(azimuth), jnp.sin(height)], axis=0)
+    ang = jnp.concatenate([ang[:, b * size:(b + 1) * size] for b in range(blocks)], axis=0)
+    odd = lax.broadcasted_iota(jnp.int32, ang.shape, 0) % 2 == 1
+    ang = jnp.where(odd, 0.5 * ang, ang)
+    cos, sin = jnp.cos(ang), jnp.sin(ang)
+    normal = []
+    for b in range(blocks):
+        cos_h = cos[2 * b + 1:2 * b + 2]
+        normal.append(jnp.concatenate(
+            [cos_h * cos[2 * b:2 * b + 1], cos_h * sin[2 * b:2 * b + 1], sin[2 * b + 1:2 * b + 2]], axis=0
+        ))
+    normal = jnp.concatenate(normal, axis=1)
     nrm[...] = normal
     area = area_ref[...]
     scaled = normal * (area * (1.0 / math.pi))
@@ -82,13 +106,8 @@
         geo[at, 6:7, :] = dist[:, lanes]
         geo[at, 7:8, :] = shift[:, lanes]
 
-    pl.semaphore_wait(barrier, len(peers) + len(mates))
-
-    mine = pl.ds(z * blocks + sub * half, half)
-    geo_in = [send(geo.at[mine], geo.at[mine], {"blk": peer}) for peer in peers]
-    vis_in = send(vis_v.at[sub], vis_v.at[sub], sibling)
-    words_in = send(occl_ref.at[pl.ds((n_sub - 1 - sub) * half, half)], words.at[sub], sibling)
-
+    for copy in field_loads:
+        copy.wait()
     bands = direct_ref.shape[0]
     row = lax.broadcasted_iota(jnp.int32, (bands, 1), 0)
     frac = jnp.zeros((bands, 1), jnp.float32)
@@ -101,8 +120,6 @@
     emitted = reflect * direct_ref[...] + (1.0 - reflect) * black
     for b in range(blocks):
         fields[0][z * blocks + b] = emitted[:, b * size:(b + 1) * size]
-    field_in = [send(fields[0].at[mine], fields[0].at[mine], {"blk": peer}) for peer in peers]
-
     for rr in range(half):
         lanes = pl.ds(pl.multiple_of((sub * half + rr) * size, size), size)
         pos_row = pos_ref[:, lanes]
@@ -123,6 +140,16 @@
         full = jnp.concatenate([hi, mid, low, hi, mid, hi, const, jnp.zeros_like(const)], axis=0)
         rhs[rr] = full.astype(jnp.bfloat16)
 
+    pl.semaphore_wait(barrier, len(peers) + len(mates))
+
+    mine = pl.ds(z * blocks + sub * half, half)
+    geo_in = [send(geo.at[mine], geo.at[mine], {"blk": peer}) for peer in peers]
+    vis_load.wait()
+    vis_in = send(vis_v.at[sub], vis_v.at[sub], sibling)
+    words_in = send(occl_ref.at[pl.ds((n_sub - 1 - sub) * half, half)], words.at[sub], sibling)
+
+    field_in = [send(fields[0].at[mine], fields[0].at[mine], {"blk": peer}) for peer in peers]
+
     def forward(copies, place):
         passed = []
         for copy, source in zip(copies, sources):
@@ -132,11 +159,12 @@
         return passed
 
     vis_in.wait_recv()
-    to_smem = pltpu.make_async_copy(vis_v, vis_s, loc_sem.at[1])
+    to_smem = pltpu.make_async_copy(vis_v, vis_s, loc_sem.at[len(loads)])
     to_smem.start()
     geo_passed = forward(geo_in, lambda region: geo.at[region])
     to_smem.wait()
-    own_words.wait()
+    for copy in late_loads:
+        copy.wait()
     words_in.wait_recv()
     for copy in geo_passed:
         copy.wait_recv()
@@ -179,7 +207,7 @@
                     w_lo[rr, at, :] = (w - top.astype(jnp.float32)).astype(jnp.bfloat16)
             return total
 
-        total = lax.fori_loop(0, slots, tile, jnp.zeros((8, size), jnp.float32))
+        total = lax.fori_loop(0, slots, tile, jnp.zeros((8, size), jnp.float32), unroll=4)
         return jnp.sum(total, axis=0, keepdims=True)
 
     totals = []
@@ -263,16 +291,25 @@
         (n_blk - 1) * 4 + 2 + (ITERS - 1) * half * (2 * (n_blk - 1) + 1) + half + n_band * n_sub - 1
     )
     vmem = pl.BlockSpec(memory_space=pltpu.VMEM)
-    smem = pl.BlockSpec(memory_space=pltpu.SMEM)
+    hbm = pl.BlockSpec(memory_space=pltpu.HBM)
     out, new_temp = pl.pallas_call(
         functools.partial(kernel, (n_blk, n_band, n_sub, blocks, listed, size)),
         out_shape=(
             jax.ShapeDtypeStruct((bands, rows), jnp.float32),
             jax.ShapeDtypeStruct((1, rows), jnp.float32),
         ),
-        in_specs=[vmem, vmem, vmem, vmem, smem, pl.BlockSpec(memory_space=pl.ANY), vmem, vmem, smem, vmem, vmem],
+        in_specs=[hbm] * 11,
         out_specs=(vmem, vmem),
         scratch_shapes=[
+            pltpu.VMEM(positions.shape, jnp.float32),
+            pltpu.VMEM(angles.shape, jnp.float32),
+            pltpu.VMEM(area.shape, jnp.float32),
+            pltpu.SMEM(counts.shape, jnp.int32),
+            pltpu.VMEM(direct.shape, jnp.float32),
+            pltpu.VMEM(reflect.shape, jnp.float32),
+            pltpu.SMEM(band_frac.shape, jnp.float32),
+            pltpu.VMEM((1, rows), jnp.float32),
+            pltpu.VMEM((1, rows), jnp.float32),
             pltpu.VMEM((total_blocks, 8, size), jnp.float32),
             pltpu.VMEM((3, rows), jnp.float32),
             pltpu.VMEM((8, 3 * size), jnp.float32),
@@ -286,11 +323,11 @@
             pltpu.VMEM((n_band, n_sub, half, size), jnp.float32),
             pltpu.SemaphoreType.DMA((copies,)),
             pltpu.SemaphoreType.DMA((copies,)),
-            pltpu.SemaphoreType.DMA((2,)),
+            pltpu.SemaphoreType.DMA((12,)),
         ]
         + [pltpu.VMEM((total_blocks, bands, size), jnp.float32)] * ITERS,
         compiler_params=pltpu.CompilerParams(
-            collective_id=0, has_side_effects=True, vmem_limit_bytes=40 * 1024 * 1024
+            collective_id=0, has_side_effects=True, vmem_limit_bytes=60 * 1024 * 1024
         ),
     )(positions, angles, area, vis_list, counts, occl, direct, reflect, band_frac, temp[None, :], heat[None, :])
     return out[:band_count], new_temp.reshape(rows)

time: 39.1 us -> 30.7 us (0.79)
  local copies, waits for them, and re-layouts: 7.81 us -> 1.97 us
  Pallas kernels: 30.1 us -> 27.8 us
    unnamed x24 -> x4, local copies, waits for them, and re-layouts: 7.81 us -> 1.97 us
    pallas_call x1, Pallas kernels: 30.1 us -> 27.8 us  [local(): pl.pallas_call(functools.partial(kernel, (n_blk, n_band, n_sub, blocks, l...]
where the time goes in v2:
time: 30.7 us; the launch traced here: 30.4 us
  Pallas kernels  27.8 us (91%)
  local copies, waits for them, and re-layouts  1.97 us (6%)
  between operations  0.65 us (2%)
    pallas_call x1, Pallas kernels, local(): pl.pallas_call(functools.partial(kernel, (n_blk, n_band, n_sub, blocks, l...  27.8 us
    unnamed x4, local copies, waits for them, and re-layouts  1.97 us

profile of v2, /device:TPU:0, one launch (start us, length us, event | category | flops | bytes accessed | tf_op | source)
XLA Modules:
  0.0 30.4 jit_solution(15700687259899749918)
XLA Ops:
  0.6 27.8 %shard_map.122 = (f32[8,1024]{1,0:T(8,128)}, f32[1,1024]{1,0:T(1,128)}) custom-call(f32[3,1024]{1,0:T(4,128)} %pos_in.1, f32[2,1024]{1,0:T(2,128)} %ang_in.1, f32[1,1024]{1,0:T(1,128)} %area_in.1, s32[4,4]{1,0:T(4,128)} %vis_ref.1, s32[4]{0:T(128)} %counts_in.1, s32[4,4,16,256]{3,2,1,0:T(8,128)} %occl_ref.1, f32[8,1024]{1,0:T(8,128)} %direct_in.1, ...), custom_call_target="tpu_custom_call" | custom-call | tf_op jit(solution)/shard_map/pallas_call | solution.py:295
  28.5 0.0 copy-start
  28.5 1.4 %copy.15 = f32[8,1024]{1,0:T(8,128)} copy(f32[8,1024]{1,0:T(8,128)} %get-tuple-element.8) | data formatting | bytes 65536
  29.8 0.0 copy-done
  29.8 0.6 %copy.16 = f32[1024]{0:T(1024)} copy(f32[1024]{0:T(1024)S(1)} %bitcast.5) | data formatting | bytes 8192
Async XLA Ops:
  28.5 1.4 %copy-start = (f32[1,1024]{1,0:T(1,128)S(1)}, f32[1,1024]{1,0:T(1,128)}, u32[]{:S(2)}) copy-start(f32[1,1024]{1,0:T(1,128)} %get-tuple-element.5) | copy-start | bytes 12292

commit v3 on v2

--- a/solution.py
+++ b/solution.py
@@ -250,17 +250,20 @@
                 gain = (1.0 - own_reflect) * (
                     direct_ref[:, lanes] + incoming - frac * (own_temp2 * own_temp2)
                 )
+                net[band, sub, rr:rr + 1, :] = jnp.sum(gain, axis=0, keepdims=True)
+                if rr == half - 1:
+                    for mate in mates:
+                        waiting.append(
+                            send(net.at[band, sub], net.at[band, sub], {"band": mate[0], "sub": mate[1]})
+                        )
                 last[sub * half + rr] = value
                 region = last.at[pl.ds(sub * half + rr, 1)]
                 waiting.append(send(region, region, sibling))
-                net[band, sub, rr:rr + 1, :] = jnp.sum(gain, axis=0, keepdims=True)
         for copy, at in hops:
             copy.wait_recv()
             region = fields[step + 1].at[pl.ds(at, 1)]
             waiting.append(send(region, region, sibling))
 
-    for mate in mates:
-        waiting.append(send(net.at[band, sub], net.at[band, sub], {"band": mate[0], "sub": mate[1]}))
     for copy in waiting:
         copy.wait_recv()
     for b in range(blocks):
@@ -272,6 +275,11 @@
         newt_ref[:, lanes] = temp_ref[:, lanes] + heat_ref[:, lanes] * flux
     for copy in started:
         copy.wait_send()
+
+
+def finish(out_in, newt_in, out_ref, newt_ref):
+    out_ref[...] = out_in[...]
+    newt_ref[...] = newt_in[...]
 
 
 def local(axes, positions, angles, area, vis_list, counts, occl, direct, reflect, band_frac, temp, heat):
@@ -330,6 +338,15 @@
             collective_id=0, has_side_effects=True, vmem_limit_bytes=60 * 1024 * 1024
         ),
     )(positions, angles, area, vis_list, counts, occl, direct, reflect, band_frac, temp[None, :], heat[None, :])
+    out, new_temp = pl.pallas_call(
+        finish,
+        out_shape=(
+            jax.ShapeDtypeStruct((bands, rows), jnp.float32),
+            jax.ShapeDtypeStruct((1, rows), jnp.float32),
+        ),
+        in_specs=[vmem, vmem],
+        out_specs=(vmem, vmem),
+    )(out, new_temp)
     return out[:band_count], new_temp.reshape(rows)
 
 

time: 30.7 us -> 30.1 us (0.980)
  local copies, waits for them, and re-layouts: 1.97 us -> 0 us
  Pallas kernels: 27.8 us -> 29.2 us
    unnamed x4 -> x0, local copies, waits for them, and re-layouts: 1.97 us -> none
    pallas_call x0 -> x1, Pallas kernels: none -> 1.38 us  [local(): pl.pallas_call(finish, out_shape=(jax.ShapeDtypeStruct((bands, rows), jnp...]
where the time goes in v3:
time: 30.1 us; the launch traced here: 29.8 us
  Pallas kernels  29.2 us (97%)
  between operations  0.64 us (2%)
    pallas_call x1, Pallas kernels, local(): pl.pallas_call(functools.partial(kernel, (n_blk, n_band, n_sub, blocks, l...  27.8 us
    pallas_call x1, Pallas kernels, local(): pl.pallas_call(finish, out_shape=(jax.ShapeDtypeStruct((bands, rows), jnp...  1.38 us

profile of v3, /device:TPU:0, one launch (start us, length us, event | category | flops | bytes accessed | tf_op | source)
XLA Modules:
  0.0 29.8 jit_solution(8437250775714414625)
XLA Ops:
  0.6 27.8 %shard_map.122 = (f32[8,1024]{1,0:T(8,128)}, f32[1,1024]{1,0:T(1,128)}) custom-call(f32[3,1024]{1,0:T(4,128)} %pos_in.1, f32[2,1024]{1,0:T(2,128)} %ang_in.1, f32[1,1024]{1,0:T(1,128)} %area_in.1, s32[4,4]{1,0:T(4,128)} %vis_ref.1, s32[4]{0:T(128)} %counts_in.1, s32[4,4,16,256]{3,2,1,0:T(8,128)} %occl_ref.1, f32[8,1024]{1,0:T(8,128)} %direct_in.1, ...), custom_call_target="tpu_custom_call" | custom-call | tf_op jit(solution)/shard_map/pallas_call | solution.py:303
  28.5 1.4 %shard_map.123 = (f32[8,1024]{1,0:T(8,128)}, f32[1,1024]{1,0:T(1,128)}) custom-call(f32[8,1024]{1,0:T(8,128)} %get-tuple-element.6.out_in, f32[1,1024]{1,0:T(1,128)} %get-tuple-element.7.newt_in), custom_call_target="tpu_custom_call" | custom-call | tf_op jit(solution)/shard_map/pallas_call | solution.py:341
